TPU v7x, 32 devices: a whole 2x2x4 slice. The times are simulated.
32 devices in a mesh: req: 16 (over z, y, x), tp: 2 (over core).
Axes of the slice: x: 2, y: 2, z: 4, core: 2. Of those that a mesh axis runs over, the one named last changes fastest.
Arguments:
- hidden_in: bfloat16 [2048, 2048], P('req')
- attn_gain: float32 [2048], replicated, may hold values from 0.1 to 1.9
- w_query: bfloat16 [2048, 2048], P(None, 'tp'), may hold values from -0.125 to 0.125
- w_keyval: bfloat16 [2048, 4, 256], P(None, 'tp'), may hold values from -0.125 to 0.125
- w_out: bfloat16 [2048, 2048], P('tp'), may hold values from -0.125 to 0.125
- moe_gain: float32 [2048], replicated, may hold values from 0.1 to 1.9
- w_gate_up: bfloat16 [16, 2, 2048, 1408], P('req', None, None, 'tp'), may hold values from -0.125 to 0.125
- w_down: bfloat16 [16, 1408, 2048], P('req', 'tp'), may hold values from -0.15625 to 0.15625
- seg_ids: int32 [16, 128], P('req'), may hold values from 0 to 3, never falling along the last dimension, each value on 1 to 64 neighbouring positions
- cached_len: int32 [16], P('req'), may hold values from 2048 to 4096, as said below
- page_table: int32 [16, 32], P('req'), may hold values from 0 to 255, as said below
- cache_pool: bfloat16 [256, 4, 128, 256], P('req', 'tp')
- expert_ids: int32 [2048, 6], P('req'), may hold values from 0 to 15, all different within a row; in each aligned block of 128 rows (0 to 127, 128 to 255, ...) at most 64 rows name the same one
- expert_weights: float32 [2048, 6], P('req'), may hold values from 0.05 to 0.5
Outputs:
- layer_out: bfloat16 [2048, 2048], P('req')
Inputs may be any that keep to these rules, and one draw needn't show every extreme that they name: `seg_ids`: row r holds the prompt numbers of pack r, never falling along the row; each prompt has 1 to 64 tokens, one exactly that many. `cached_len`: some pack has exactly 4096 cached tokens. `page_table`: entry j of row r names the page holding tokens j * 128 to (j + 1) * 128 - 1 of pack r's cached prefix; page p lies on index p // 16 of req. At most 4 entries of one row lie on one owner, and in every row some owner holds exactly 4. Entries past the cached length name pages too. `expert_ids`: each row names 6 different experts. Among the rows of one pack no expert is named more than 64 times, a bound that some block reaches.
All inputs are finite; a program needn't handle non-finite values.
Results may differ from a plain program's by a relative error of at most 0.009.
Values may be sent and summed in bfloat16 or wider, within the bound.
A program may use at most 128 MiB of HBM per device.

v0:
```python
import math

import jax
import jax.numpy as jnp
from jax import lax
from jax.sharding import PartitionSpec as P

eps = 1e-06
rope_base = 600000.0


def rms_scale(rows_in, gain):
    widened = rows_in.astype(jnp.float32)
    return widened * lax.rsqrt(jnp.mean(widened * widened, axis=-1, keepdims=True) + eps) * gain


def rotate(vectors, angles):
    half_dim = vectors.shape[-1] // 2
    first_half = vectors[..., :half_dim]
    second_half = vectors[..., half_dim:]
    cosine = jnp.cos(angles)[:, None, :]
    sine_vals = jnp.sin(angles)[:, None, :]
    return jnp.concatenate(
        [
            first_half * cosine - second_half * sine_vals,
            second_half * cosine + first_half * sine_vals,
        ],
        axis=-1,
    )


def positions(segment_row, cached):
    length = segment_row.shape[0]
    token_index = jnp.arange(length, dtype=jnp.int32)
    begins = jnp.concatenate([jnp.ones((1,), dtype=bool), segment_row[1:] != segment_row[:-1]])
    seg_start = lax.cummax(jnp.where(begins, token_index, 0), axis=0)
    carried = segment_row == segment_row[0]
    place = token_index - seg_start + jnp.where(carried, cached, 0)
    return (place, carried)


def make_angles(place, head_dim):
    inverse = rope_base ** (-(jnp.arange(head_dim // 2, dtype=jnp.float32) * 2.0 / head_dim))
    return place.astype(jnp.float32)[:, None] * inverse[None, :]


def admit(segment_row, carried, cached, prefix_len):
    length = segment_row.shape[0]
    token_index = jnp.arange(length, dtype=jnp.int32)
    prefix_ok = (jnp.arange(prefix_len, dtype=jnp.int32)[None, :] < cached) & carried[:, None]
    local_ok = (segment_row[:, None] == segment_row[None, :]) & (
        token_index[None, :] <= token_index[:, None]
    )
    return jnp.concatenate([prefix_ok, local_ok], axis=1)


def attend(queries, all_keys, all_values, admitted):
    scale = 1.0 / math.sqrt(queries.shape[-1])
    scores = (
        jnp.einsum("tkgd,knd->kgtn", queries, all_keys, preferred_element_type=jnp.float32) * scale
    )
    scores = jnp.where(admitted[None, None], scores, -1e30)
    highest = jnp.max(scores, axis=-1, keepdims=True)
    expo = jnp.exp(scores - highest)
    totals = jnp.sum(expo, axis=-1, keepdims=True)
    weights = (expo / totals).astype(jnp.bfloat16)
    context = jnp.einsum("kgtn,knd->tkgd", weights, all_values, preferred_element_type=jnp.float32)
    return context.astype(jnp.bfloat16)


def shards(
    hidden_in,
    attn_gain,
    w_query,
    w_keyval,
    w_out,
    moe_gain,
    w_gate_up,
    w_down,
    seg_ids,
    cached_len,
    page_table,
    cache_pool,
    expert_ids,
    expert_weights,
):
    tok_rows, model_width = hidden_in.shape
    head_dim = w_keyval.shape[2] // 2
    kv_local = w_keyval.shape[1]
    q_local = w_query.shape[1] // head_dim
    group_size = q_local // kv_local
    segment_row = seg_ids[0]
    cached = cached_len[0]
    place, carried = positions(segment_row, cached)
    angles = make_angles(place, head_dim)
    normed = rms_scale(hidden_in, attn_gain).astype(jnp.bfloat16)
    n_req = lax.axis_size("req")
    listed = page_table[0]
    pref_pages = listed.shape[0]
    pages_dev = cache_pool.shape[0]
    page_len = cache_pool.shape[2]
    cap_pages = (2 * pref_pages + n_req - 1) // n_req
    owners = listed // pages_dev
    entry_index = jnp.arange(pref_pages, dtype=jnp.int32)
    earlier = (owners[None, :] == owners[:, None]) & (entry_index[None, :] < entry_index[:, None])
    owner_rank = jnp.sum(earlier.astype(jnp.int32), axis=1)
    page_slot = listed % pages_dev
    cap_index = jnp.arange(cap_pages, dtype=jnp.int32)
    owner_index = jnp.arange(n_req, dtype=jnp.int32)
    wanted = (owners[None, None, :] == owner_index[:, None, None]) & (
        owner_rank[None, None, :] == cap_index[None, :, None]
    )
    request = jnp.sum(jnp.where(wanted, page_slot[None, None, :], 0), axis=2)
    asked_slots = lax.all_to_all(request, "req", split_axis=0, concat_axis=0, tiled=True)
    served = cache_pool[asked_slots.reshape(-1)].reshape(
        n_req, cap_pages, kv_local, page_len, 2 * head_dim
    )
    fetched = lax.all_to_all(served, "req", split_axis=0, concat_axis=0, tiled=True)
    fetched = fetched.reshape(n_req * cap_pages, kv_local, page_len, 2 * head_dim)[
        owners * cap_pages + owner_rank
    ]
    prefix = jnp.transpose(fetched, (1, 0, 2, 3)).reshape(
        kv_local, pref_pages * page_len, 2 * head_dim
    )
    queries = jnp.dot(normed, w_query, preferred_element_type=jnp.float32).reshape(
        tok_rows, q_local, head_dim
    )
    queries = (
        rotate(queries, angles)
        .astype(jnp.bfloat16)
        .reshape(tok_rows, kv_local, group_size, head_dim)
    )
    keyval = jnp.dot(
        normed,
        w_keyval.reshape(model_width, kv_local * 2 * head_dim),
        preferred_element_type=jnp.float32,
    ).reshape(tok_rows, kv_local, 2 * head_dim)
    keys_new = rotate(keyval[..., :head_dim], angles).astype(jnp.bfloat16)
    values_new = keyval[..., head_dim:].astype(jnp.bfloat16)
    all_keys = jnp.concatenate([prefix[..., :head_dim], jnp.transpose(keys_new, (1, 0, 2))], axis=1)
    all_values = jnp.concatenate(
        [prefix[..., head_dim:], jnp.transpose(values_new, (1, 0, 2))], axis=1
    )
    admitted = admit(segment_row, carried, cached, pref_pages * page_len)
    context = attend(queries, all_keys, all_values, admitted).reshape(tok_rows, q_local * head_dim)
    attention = lax.psum(jnp.dot(context, w_out, preferred_element_type=jnp.float32), "tp")
    resid = (hidden_in.astype(jnp.float32) + attention).astype(jnp.bfloat16)
    moe_in = rms_scale(resid, moe_gain).astype(jnp.bfloat16)
    topk = expert_ids.shape[1]
    n_exp = n_req * w_gate_up.shape[0]
    cap_e = 4 * tok_rows * topk // (3 * n_exp)
    flat_ids = expert_ids.reshape(-1)
    onehot = (flat_ids[:, None] == jnp.arange(n_exp, dtype=jnp.int32)[None, :]).astype(jnp.int32)
    slot_rank = jnp.sum((jnp.cumsum(onehot, axis=0) - 1) * onehot, axis=1)
    assign_slot = flat_ids * cap_e + slot_rank
    slot_match = assign_slot[None, :] == jnp.arange(n_exp * cap_e, dtype=jnp.int32)[:, None]
    selector = jnp.any(slot_match.reshape(n_exp * cap_e, tok_rows, topk), axis=2).astype(
        jnp.bfloat16
    )
    outgoing = (
        jnp.dot(selector, moe_in, preferred_element_type=jnp.float32)
        .astype(jnp.bfloat16)
        .reshape(n_exp, cap_e, model_width)
    )
    expert_in = lax.all_to_all(outgoing, "req", split_axis=0, concat_axis=0, tiled=True)
    expert_rows = expert_in.reshape(-1, model_width)
    gate_part = jnp.dot(expert_rows, w_gate_up[0, 0], preferred_element_type=jnp.float32)
    up_part = jnp.dot(expert_rows, w_gate_up[0, 1], preferred_element_type=jnp.float32)
    hidden_act = (jax.nn.silu(gate_part) * up_part).astype(jnp.bfloat16)
    expert_share = lax.psum_scatter(
        jnp.dot(hidden_act, w_down[0], preferred_element_type=jnp.float32).astype(jnp.bfloat16),
        "tp",
        scatter_dimension=0,
        tiled=True,
    )
    whole_rows = lax.all_gather(expert_share, "tp", axis=0, tiled=True)
    results = lax.all_to_all(
        whole_rows.reshape(-1, cap_e, model_width), "req", split_axis=0, concat_axis=0, tiled=True
    )
    picked = results.reshape(-1, model_width)[assign_slot].reshape(tok_rows, topk, model_width)
    moe_out = jnp.sum(expert_weights[:, :, None] * picked.astype(jnp.float32), axis=1)
    return (resid.astype(jnp.float32) + moe_out).astype(jnp.bfloat16)


def solution(mesh):
    in_specs = (
        P("req", None),
        P(),
        P(None, "tp"),
        P(None, "tp", None),
        P("tp", None),
        P(),
        P("req", None, None, "tp"),
        P("req", "tp", None),
        P("req", None),
        P("req"),
        P("req", None),
        P("req", "tp", None, None),
        P("req", None),
        P("req", None),
    )
    out_specs = P("req", None)
    return jax.shard_map(shards, mesh=mesh, in_specs=in_specs, out_specs=out_specs, check_vma=False)
```

profile of v0, /device:TPU:15, one launch (start us, length us, event | category | flops | bytes accessed | tf_op | source)
XLA Modules:
  0.0 565.8 jit_solution(17048353428292019175)
XLA Ops:
  8.5 9.6 %all_to_all.24 = s32[16,1,4]{2,1,0:T(1,128)S(1)} all-to-all(s32[16,1,4]{2,1,0:T(1,128)S(1)} %copy.50), channel_id=1, replica_groups=mesh['req'=16,'tp'=2] {'req'}, dimensions={0} | all-to-all | bytes 512 | tf_op jit(solution)/shard_map/all_to_all | solution.py:114
  19.4 7.0 %gather_fusion = bf16[64,2,128,256]{3,2,1,0:T(8,128)(2,1)} fusion(bf16[16,2,128,256]{3,2,1,0:T(8,128)(2,1)} %param.25, s32[1024]{0:T(1024)S(1)} %pad_clamp_fusion.2), kind=kCustom, calls=%fused_computation | custom fusion | bytes 16777472 | tf_op jit(solution)/shard_map/gather | solution.py:115
  26.4 7.6 %all-to-all-start.1 = ((bf16[16,4,2,128,256]{4,3,2,1,0:T(8,128)(2,1)}), bf16[16,4,2,128,256]{4,3,2,1,0:T(8,128)(2,1)}, u32[]{:S(2)}, u32[]{:S(2)}) async-start(bf16[16,4,2,128,256]{4,3,2,1,0:T(8,128)(2,1)} %bitcast.129), calls=%async_computation.1 | async-start | bytes 16777216 | tf_op jit(solution)/shard_map/all_to_all | solution.py:118
  35.3 3.4 copy.70
  38.7 4.0 copy.52
  42.9 3.1 convolution_bitcast_fusion
  52.5 167.6 %all-to-all-done.1 = bf16[16,4,2,128,256]{4,3,2,1,0:T(8,128)(2,1)} async-done(((bf16[16,4,2,128,256]{4,3,2,1,0:T(8,128)(2,1)}), bf16[16,4,2,128,256]{4,3,2,1,0:T(8,128)(2,1)}, u32[]{:S(2)}, u32[]{:S(2)}) %all-to-all-start.1) | async-done | bytes 8388640 | tf_op jit(solution)/shard_map/all_to_all | solution.py:118
  220.1 6.2 %gather_fusion.1 = bf16[32,2,128,256]{3,2,1,0:T(8,128)(2,1)} fusion(bf16[64,2,128,256]{3,2,1,0:T(8,128)(2,1)} %bitcast.5, s32[1024]{0:T(1024)S(1)} %pad_clamp_fusion.1), kind=kCustom, calls=%fused_computation.1 | custom fusion | bytes 8388736 | tf_op jit(solution)/shard_map/gather | solution.py:119
  226.3 2.5 copy.51
  229.8 8.4 %fusion.16 = f32[2,4224,128,4]{2,1,3,0:T(8,128)} fusion(bf16[2,128,128]{2,1,0:T(8,128)(2,1)S(1)} %maximum_bitcast_fusion.6, bf16[2,4096,128]{2,1,0:T(8,128)(2,1)S(1)} %get-tuple-element.10, bf16[128,2,4,64]{3,0,2,1:T(8,128)(2,1)S(1)} %bitcast.141, bf16[128,2,4,64]{3,0,2,1:T(8,128)(2,1)S(1)} %bitcast.140), kind=kOutput, calls=%fused_computation.29 | convolution fusion | flops 1112145920 | bytes 19726336 | tf_op jit(solution)/shard_map/tkgd,knd->kgtn/dot_general | solution.py:60
  238.2 13.3 %fusion.60 = (f32[2,4,128]{2,1,0:T(4,128)S(1)}, f32[2,4,128,4224]{2,3,1,0:T(8,128)}) fusion(f32[2,4224,128,4]{2,1,3,0:T(8,128)} %fusion.16, pred[128,4224]{0,1:T(8,128)(4,1)S(1)} %copy-done.3), kind=kOutput, calls=%fused_computation.124 | output fusion | flops 17305728 | bytes 35147776 | tf_op jit(solution)/shard_map/sub | solution.py:64
  251.5 7.9 %fusion.21 = bf16[2,128,4,128]{3,1,2,0:T(8,128)(2,1)S(1)} fusion(f32[2,4,128,4224]{2,3,1,0:T(8,128)} %get-tuple-element.22, f32[2,4,128]{2,1,0:T(4,128)S(1)} %get-tuple-element.21, bf16[2,128,128]{2,1,0:T(8,128)(2,1)S(1)} %fusion.42, bf16[2,4096,128]{2,1,0:T(8,128)(2,1)S(1)} %get-tuple-element.9), kind=kOutput, calls=%fused_computation.40 | convolution fusion | flops 1120403456 | bytes 19730432 | tf_op jit(solution)/shard_map/kgtn,knd->tkgd/dot_general | solution.py:67
  262.3 3.2 reduce-window.19
  268.7 15.7 %all-reduce.2.cloned.1.call-done = f32[128,2048]{1,0:T(8,128)} async-done(((f32[128,2048]{1,0:T(8,128)}), f32[128,2048]{1,0:T(8,128)}) %all-reduce.2.cloned.1.call-update) | async-done | bytes 1048592 | tf_op jit(solution)/shard_map/psum | solution.py:146
  287.3 97.6 %all_to_all.25 = bf16[16,64,2048]{2,1,0:T(8,128)(2,1)S(1)} all-to-all(bf16[16,64,2048]{2,1,0:T(8,128)(2,1)S(1)} %bitcast.132), channel_id=1, replica_groups=mesh['req'=16,'tp'=2] {'req'}, dimensions={0} | all-to-all | bytes 8388608 | tf_op jit(solution)/shard_map/all_to_all | solution.py:165
  386.9 4.8 fusion.8
  391.7 11.3 %convolution_convert_fusion = bf16[1024,2048]{1,0:T(8,128)(2,1)} fusion(bf16[1,704,2048]{2,1,0:T(8,128)(2,1)S(1)} %copy-done, f32[1024,704]{0,1:T(8,128)} %fusion.8, bf16[1024,2048]{1,0:T(8,128)(2,1)} %bitcast.138, bf16[1,2,2048,704]{2,3,1,0:T(8,128)(2,1)} %param.20), kind=kOutput, calls=%fused_computation.13 | convolution fusion | flops 5912002560 | bytes 17039360 | tf_op jit(solution)/shard_map/dot_general | solution.py:171
  403.1 13.8 %reduce-scatter.2.cloned.1.call-done = bf16[512,2048]{1,0:T(8,128)(2,1)} async-done(((bf16[1024,2048]{1,0:T(8,128)(2,1)}), bf16[512,2048]{1,0:T(8,128)(2,1)}) %reduce-scatter.2.cloned.1.call-update) | async-done | bytes 2097168 | tf_op jit(solution)/shard_map/reduce_scatter | solution.py:170
  416.9 16.6 %all-gather.2.cloned.1.call-done = bf16[1024,2048]{1,0:T(8,128)(2,1)} async-done(((bf16[512,2048]{1,0:T(8,128)(2,1)}), bf16[1024,2048]{1,0:T(8,128)(2,1)}) %all-gather.2.cloned.1.call-update) | async-done | bytes 4194320 | tf_op jit(solution)/shard_map/all_gather | solution.py:176
  433.5 6.5 %all-to-all-start.3 = ((bf16[16,64,2048]{2,1,0:T(8,128)(2,1)}), bf16[16,64,2048]{2,1,0:T(8,128)(2,1)}, u32[]{:S(2)}, u32[]{:S(2)}) async-start(bf16[16,64,2048]{2,1,0:T(8,128)(2,1)} %bitcast.136), calls=%async_computation.4 | async-start | bytes 8388608 | tf_op jit(solution)/shard_map/all_to_all | solution.py:177
  440.3 95.0 %all-to-all-done.3 = bf16[16,64,2048]{2,1,0:T(8,128)(2,1)} async-done(((bf16[16,64,2048]{2,1,0:T(8,128)(2,1)}), bf16[16,64,2048]{2,1,0:T(8,128)(2,1)}, u32[]{:S(2)}, u32[]{:S(2)}) %all-to-all-start.3) | async-done | bytes 4194336 | tf_op jit(solution)/shard_map/all_to_all | solution.py:177
  535.3 9.8 %gather_fusion.2 = bf16[768,2048]{1,0:T(8,128)(2,1)} fusion(bf16[1024,2048]{1,0:T(8,128)(2,1)} %bitcast.35, s32[1024]{0:T(1024)S(1)} %pad_clamp_fusion), kind=kCustom, calls=%fused_computation.2 | custom fusion | bytes 6294528 | tf_op jit(solution)/shard_map/gather | solution.py:180
  545.1 6.6 %reshape.502 = f32[128,6,2048]{2,1,0:T(8,128)} reshape(bf16[768,2048]{1,0:T(8,128)(2,1)} %gather_fusion.2) | data formatting | bytes 9437184 | tf_op jit(solution)/shard_map/convert_element_type | solution.py:181
  551.6 6.7 %multiply_reduce_fusion = f32[128,2048]{1,0:T(8,128)S(1)} fusion(f32[128,6,2048]{2,1,0:T(8,128)} %reshape.502, f32[128,6]{1,0:T(8,128)S(1)} %copy.58), kind=kLoop, calls=%fused_computation.12 | loop fusion | flops 2883584 | bytes 7343104 | tf_op jit(solution)/shard_map/reduce_sum | solution.py:181
  (102 shorter events, 23.6 us)
Async XLA Ops:
  6.5 385.2 %copy-start = (bf16[1,704,2048]{2,1,0:T(8,128)(2,1)S(1)}, bf16[1,704,2048]{2,1,0:T(8,128)(2,1)}, u32[]{:S(2)}) copy-start(bf16[1,704,2048]{2,1,0:T(8,128)(2,1)} %param.21) | copy-start | bytes 8650756
  26.4 8.3 %copy-start.13 = (s32[1,128]{1,0:T(1,128)S(1)}, s32[1,128]{1,0:T(1,128)}, u32[]{:S(2)}) copy-start(s32[1,128]{1,0:T(1,128)} %param.22) | copy-start | bytes 1540
  26.4 193.7 %all-to-all-start.1 = ((bf16[16,4,2,128,256]{4,3,2,1,0:T(8,128)(2,1)}), bf16[16,4,2,128,256]{4,3,2,1,0:T(8,128)(2,1)}, u32[]{:S(2)}, u32[]{:S(2)}) async-start(bf16[16,4,2,128,256]{4,3,2,1,0:T(8,128)(2,1)} %bitcast.129), calls=%async_computation.1 | async-start | bytes 16777216 | tf_op jit(solution)/shard_map/all_to_all | solution.py:118
  34.0 250.4 %all-reduce.2.cloned.1.call-start = ((), (), s32[]{:S(2)}) async-start(), calls=%async_computation.5 | async-start | bytes 2097152 | tf_op jit(solution)/shard_map/psum | solution.py:146
  35.3 7.4 %copy-start.2 = (bf16[128,2048]{1,0:T(8,128)(2,1)S(1)}, bf16[128,2048]{1,0:T(8,128)(2,1)}, u32[]{:S(2)}) copy-start(bf16[128,2048]{1,0:T(8,128)(2,1)} %param.14) | copy-start | bytes 1572868
  35.3 7.6 %copy-start.11 = (f32[2048]{0:T(1024)S(1)}, f32[2048]{0:T(1024)}, u32[]{:S(2)}) copy-start(f32[2048]{0:T(1024)} %param.15) | copy-start | bytes 24580
  42.9 5.4 copy-start.16
  42.9 5.4 copy-start.1
  228.8 1.0 copy-start.8
  228.8 1.0 copy-start.9
  229.8 8.4 %copy-start.3 = (pred[128,4224]{0,1:T(8,128)(4,1)S(1)}, pred[128,4224]{0,1:T(8,128)(4,1)}, u32[]{:S(2)}) copy-start(pred[128,4224]{0,1:T(8,128)(4,1)} %pad_add_fusion) | copy-start | bytes 1622020
  251.5 7.9 %copy-start.6 = (bf16[1024,2048]{1,0:T(8,128)(2,1)S(1)}, bf16[1024,2048]{1,0:T(8,128)(2,1)}, u32[]{:S(2)}) copy-start(bf16[1024,2048]{1,0:T(8,128)(2,1)} %param.18) | copy-start | bytes 12582916
  259.4 1.9 copy-start.14
  259.4 26.5 %copy-start.12 = (f32[2048]{0:T(1024)S(1)}, f32[2048]{0:T(1024)}, u32[]{:S(2)}) copy-start(f32[2048]{0:T(1024)} %param.19) | copy-start | bytes 24580
  261.3 155.6 %reduce-scatter.2.cloned.1.call-start = ((), (), s32[]{:S(2)}) async-start(), calls=%async_computation.6 | async-start | bytes 6291456 | tf_op jit(solution)/shard_map/reduce_scatter | solution.py:170
  285.9 99.0 %copy-start.4 = (bf16[128,2048]{1,0:T(8,128)(2,1)}, bf16[128,2048]{1,0:T(8,128)(2,1)S(1)}, u32[]{:S(2)}) copy-start(bf16[128,2048]{1,0:T(8,128)(2,1)S(1)} %get-tuple-element.6) | copy-start | bytes 1572868
  286.0 100.9 %slice-start = ((s8[5767168]{0:T(1024)(128)(4,1)}), s8[4194304]{0:T(1024)(128)(4,1)S(1)}, s32[]{:S(2)}) async-start(s8[5767168]{0:T(1024)(128)(4,1)} %bitcast.147), calls=%async_computation.8 | async-start | bytes 8388608
  287.3 99.6 %slice-start.1 = ((s8[5767168]{0:T(1024)(128)(4,1)}), s8[1572864]{0:T(1024)(128)(4,1)S(1)}, s32[]{:S(2)}) async-start(s8[5767168]{0:T(1024)(128)(4,1)} %bitcast.147), calls=%async_computation.9 | async-start | bytes 3145728
  384.9 2.0 copy-start.7
  403.0 30.4 %all-gather.2.cloned.1.call-start = ((), (), s32[]{:S(2)}) async-start(), calls=%async_computation.7 | async-start | bytes 6291456 | tf_op jit(solution)/shard_map/all_gather | solution.py:176
  433.5 6.5 %copy-start.10 = (s32[128,6]{1,0:T(8,128)S(1)}, s32[128,6]{1,0:T(8,128)}, u32[]{:S(2)}) copy-start(s32[128,6]{1,0:T(8,128)} %get-tuple-element.15) | copy-start | bytes 9220
  433.5 6.7 %copy-start.15 = (f32[128,6]{0,1:T(8,128)S(1)}, f32[128,6]{0,1:T(8,128)}, u32[]{:S(2)}) copy-start(f32[128,6]{0,1:T(8,128)} %param.27) | copy-start | bytes 9220
  433.5 101.8 %all-to-all-start.3 = ((bf16[16,64,2048]{2,1,0:T(8,128)(2,1)}), bf16[16,64,2048]{2,1,0:T(8,128)(2,1)}, u32[]{:S(2)}, u32[]{:S(2)}) async-start(bf16[16,64,2048]{2,1,0:T(8,128)(2,1)} %bitcast.136), calls=%async_computation.4 | async-start | bytes 8388608 | tf_op jit(solution)/shard_map/all_to_all | solution.py:177
  551.6 6.7 %copy-start.5 = (bf16[128,2048]{1,0:T(8,128)(2,1)S(1)}, bf16[128,2048]{1,0:T(8,128)(2,1)}, u32[]{:S(2)}) copy-start(bf16[128,2048]{1,0:T(8,128)(2,1)} %copy-done.4) | copy-start | bytes 1572868
Sparse Core Ops, SparseCore 0:
  261.4 23.0 all-reduce.1
  403.2 13.6 reduce-scatter.1
  418.4 14.9 all-gather.1
where the time goes:
time: 567 us; the launch traced here: 566 us
  waiting for transfers between devices  309 us (54%)
  blocking collectives  107 us (19%)
  local copies, waits for them, and re-layouts  46.5 us (8%)
  matrix products  39.5 us (7%)
  other arithmetic  35.4 us (6%)
  starting transfers between devices  14.3 us (3%)
  between operations  14.1 us (2%)
    all_to_all x1, waiting for transfers between devices, shards(): lax.all_to_all(served, 'req', split_axis=0, concat_axis=0, tiled=True)  168 us
    all_to_all x1, blocking collectives, shards(): lax.all_to_all(outgoing, 'req', split_axis=0, concat_axis=0, tiled=True)  97.6 us
    all_to_all x1, waiting for transfers between devices, shards(): lax.all_to_all(whole_rows.reshape(-1, cap_e, model_width), 'req', split_a...  95 us
    all_gather x1, waiting for transfers between devices, shards(): whole_rows = lax.all_gather(expert_share, 'tp', axis=0, tiled=True)  16.6 us
    psum x1, waiting for transfers between devices, shards(): lax.psum(jnp.dot(context, w_out, preferred_element_type=jnp.float32), 'tp')  15.7 us
    reduce_scatter x1, waiting for transfers between devices, shards(): lax.psum_scatter(jnp.dot(hidden_act, w_down[0], preferred_element_type=jn...  13.8 us
    sub x1, other arithmetic, attend(): expo = jnp.exp(scores - highest)  13.3 us
  transfers between devices with their start and end apart: 5, of which 5 were waited for; matrix products, arithmetic and copies ran while one was open for 4% of the time, Pallas kernels for 0%

commit v1 on v0

v1 whole, which is shorter than its diff:
```python
import functools
import math

import jax
import jax.numpy as jnp
from jax import lax
from jax.experimental import pallas as pl
from jax.experimental.pallas import tpu as pltpu
from jax.sharding import PartitionSpec as P

eps = 1e-06
rope_base = 600000.0
bf16 = jnp.bfloat16
f32 = jnp.float32
far = -1e30


def push_kernel(axis, n, scatter, place, count, *refs):
    ins, outs = refs[:count], refs[count : 2 * count]
    send, recv, own = refs[2 * count :]
    me = lax.axis_index(axis)
    barrier = pltpu.get_barrier_semaphore()
    for d in range(1, n):
        pl.semaphore_signal(
            barrier,
            inc=1,
            device_id={axis: lax.rem(me + d, n)},
            device_id_type=pl.DeviceIdType.MESH,
        )
    pl.semaphore_wait(barrier, n - 1)

    def source(x, p):
        if scatter == "lead":
            return x.at[p]
        if scatter == "cols":
            width = x.shape[-1] // n
            return x.at[:, pl.ds(pl.multiple_of(p * width, 128), width)]
        return x

    def target(o):
        if place == "cols":
            width = o.shape[-1] // n
            return o.at[:, pl.ds(pl.multiple_of(me * width, 128), width)]
        return o.at[me]

    copies = []
    for d in range(1, n):
        p = lax.rem(me + d, n)
        for k in range(count):
            c = pltpu.make_async_remote_copy(
                src_ref=source(ins[k], p),
                dst_ref=target(outs[k]),
                send_sem=send.at[k, d],
                recv_sem=recv.at[k, d],
                device_id={axis: p},
                device_id_type=pl.DeviceIdType.MESH,
            )
            c.start()
            copies.append(c)
    mine = []
    for k in range(count):
        c = pltpu.make_async_copy(source(ins[k], me), target(outs[k]), own.at[k])
        c.start()
        mine.append(c)
    for c in mine:
        c.wait()
    for c in copies:
        c.wait()


def push(xs, axis, ident, scatter=None, place="lead"):
    n = lax.axis_size(axis)
    count = len(xs)
    shapes = []
    for x in xs:
        block = x.shape
        if scatter == "lead":
            block = block[1:]
        if scatter == "cols":
            block = block[:-1] + (block[-1] // n,)
        whole = block[:-1] + (block[-1] * n,) if place == "cols" else (n,) + block
        shapes.append(jax.ShapeDtypeStruct(whole, x.dtype))
    return pl.pallas_call(
        functools.partial(push_kernel, axis, n, scatter, place, count),
        out_shape=shapes,
        in_specs=[pl.BlockSpec(memory_space=pl.ANY)] * count,
        out_specs=[pl.BlockSpec(memory_space=pl.ANY)] * count,
        scratch_shapes=[
            pltpu.SemaphoreType.DMA((count, n)),
            pltpu.SemaphoreType.DMA((count, n)),
            pltpu.SemaphoreType.DMA((count,)),
        ],
        compiler_params=pltpu.CompilerParams(collective_id=ident, has_side_effects=True),
        name="push_%d" % ident,
    )(*xs)


def owner_kernel(cap, kv, scale, slot_ref, valid_ref, q_ref, pool_ref, o_ref, stat_ref):
    p = pl.program_id(0)
    page = pool_ref.shape[2]
    hd = q_ref.shape[-1]
    rows = q_ref.shape[2]
    index = lax.broadcasted_iota(jnp.int32, (page, rows), 0)
    stat_ref[...] = jnp.zeros_like(stat_ref)
    for g in range(kv):
        q = q_ref[0, g]
        tops, scores = [], []
        for c in range(cap):
            keys = pool_ref[slot_ref[p, c], g, :, :hd]
            s = lax.dot_general(keys, q, (((1,), (1,)), ((), ())), preferred_element_type=f32)
            s = jnp.where(index < valid_ref[p, c], s * scale, far)
            scores.append(s)
            tops.append(jnp.max(s, axis=0, keepdims=True))
        top = functools.reduce(jnp.maximum, tops)
        total = jnp.zeros((1, rows), f32)
        acc = jnp.zeros((hd, rows), f32)
        for c in range(cap):
            e = jnp.where(index < valid_ref[p, c], jnp.exp(scores[c] - top), 0.0)
            total += jnp.sum(e, axis=0, keepdims=True)
            values = pool_ref[slot_ref[p, c], g, :, hd:]
            acc += lax.dot_general(
                values, e.astype(bf16), (((0,), (0,)), ((), ())), preferred_element_type=f32
            )
        o_ref[0, g] = (acc / jnp.where(total > 0, total, 1.0)).astype(bf16)
        stat_ref[0, 2 * g : 2 * g + 1] = top
        stat_ref[0, 2 * g + 1 : 2 * g + 2] = total


def owner_attend(slots, valid, q_all, pool):
    n, kv, rows, hd = q_all.shape
    cap = slots.shape[1]
    lines = -(-2 * kv // 8) * 8
    return pl.pallas_call(
        functools.partial(owner_kernel, cap, kv, 1.0 / math.sqrt(hd)),
        out_shape=[
            jax.ShapeDtypeStruct((n, kv, hd, rows), bf16),
            jax.ShapeDtypeStruct((n, lines, rows), f32),
        ],
        grid_spec=pltpu.PrefetchScalarGridSpec(
            num_scalar_prefetch=2,
            grid=(n,),
            in_specs=[
                pl.BlockSpec((1, kv, rows, hd), lambda p, *_: (p, 0, 0, 0)),
                pl.BlockSpec(pool.shape, lambda p, *_: (0, 0, 0, 0)),
            ],
            out_specs=[
                pl.BlockSpec((1, kv, hd, rows), lambda p, *_: (p, 0, 0, 0)),
                pl.BlockSpec((1, lines, rows), lambda p, *_: (p, 0, 0)),
            ],
        ),
        compiler_params=pltpu.CompilerParams(vmem_limit_bytes=40 * 2**20),
        name="owner_attend",
    )(slots, valid, q_all, pool)


def merge_kernel(n, kv, group, scale, q_ref, k_ref, v_ref, ok_ref, o_ref, stat_ref, out_ref):
    hd = k_ref.shape[-1]
    rows = q_ref.shape[2]
    half = rows // group
    for h in range(2):
        ok = ok_ref[h] > 0
        for g in range(kv):
            s = lax.dot_general(
                k_ref[g], q_ref[h, g], (((1,), (1,)), ((), ())), preferred_element_type=f32
            )
            s = jnp.where(ok, s * scale, far)
            top = jnp.max(s, axis=0, keepdims=True)
            if h == 0:
                flag = ok_ref[2, 0:1] > 0
                sums = [jnp.where(flag, stat_ref[i, 2 * g + 1 : 2 * g + 2], 0.0) for i in range(n)]
                tops = [
                    jnp.where(sums[i] > 0, stat_ref[i, 2 * g : 2 * g + 1], far) for i in range(n)
                ]
                top = functools.reduce(jnp.maximum, tops, top)
            e = jnp.where(ok, jnp.exp(s - top), 0.0)
            total = jnp.sum(e, axis=0, keepdims=True)
            acc = lax.dot_general(
                v_ref[g], e.astype(bf16), (((0,), (0,)), ((), ())), preferred_element_type=f32
            )
            if h == 0:
                for i in range(n):
                    share = jnp.exp(tops[i] - top) * sums[i]
                    total += share
                    acc += share * o_ref[i, g].astype(f32)
            context = (acc / total).T.astype(bf16)
            for j in range(group):
                head = g * group + j
                out_ref[h * half : (h + 1) * half, head * hd : (head + 1) * hd] = context[
                    j * half : (j + 1) * half
                ]


def merge(q_halves, keys, values, ok, shares, stats, group):
    n, kv, hd, rows = shares.shape
    tokens = 2 * rows // group
    return pl.pallas_call(
        functools.partial(merge_kernel, n, kv, group, 1.0 / math.sqrt(hd)),
        out_shape=jax.ShapeDtypeStruct((tokens, kv * group * hd), bf16),
        in_specs=[pl.BlockSpec(memory_space=pltpu.VMEM)] * 6,
        out_specs=pl.BlockSpec(memory_space=pltpu.VMEM),
        compiler_params=pltpu.CompilerParams(vmem_limit_bytes=40 * 2**20),
        name="merge",
    )(q_halves, keys, values, ok, shares, stats)


def rms_scale(rows_in, gain):
    widened = rows_in.astype(f32)
    return widened * lax.rsqrt(jnp.mean(widened * widened, axis=-1, keepdims=True) + eps) * gain


def rotate(vectors, angles):
    half_dim = vectors.shape[-1] // 2
    a, b = vectors[..., :half_dim], vectors[..., half_dim:]
    cosine, sine = jnp.cos(angles)[:, None, :], jnp.sin(angles)[:, None, :]
    return jnp.concatenate([a * cosine - b * sine, b * cosine + a * sine], axis=-1)


def shards(
    hidden_in,
    attn_gain,
    w_query,
    w_keyval,
    w_out,
    moe_gain,
    w_gate_up,
    w_down,
    seg_ids,
    cached_len,
    page_table,
    cache_pool,
    expert_ids,
    expert_weights,
):
    tok_rows, width = hidden_in.shape
    hd = w_keyval.shape[2] // 2
    kv = w_keyval.shape[1]
    q_local = w_query.shape[1] // hd
    group = q_local // kv
    half = tok_rows // 2
    n_req, n_tp = lax.axis_size("req"), lax.axis_size("tp")
    tp_me, req_me = lax.axis_index("tp"), lax.axis_index("req")
    part = width // n_tp
    seg, cached = seg_ids[0], cached_len[0]
    token = jnp.arange(tok_rows, dtype=jnp.int32)
    start = jnp.sum((seg[None, :] < seg[:, None]).astype(jnp.int32), axis=1)
    carried = seg == seg[0]
    place = token - start + jnp.where(carried, cached, 0)
    inverse = rope_base ** (-(jnp.arange(hd // 2, dtype=f32) * 2.0 / hd))
    angles = place.astype(f32)[:, None] * inverse[None, :]

    normed = rms_scale(hidden_in, attn_gain).astype(bf16)
    queries = jnp.dot(normed, w_query, preferred_element_type=f32).reshape(tok_rows, q_local, hd)
    queries = rotate(queries, angles).astype(bf16).reshape(2, half, kv, group, hd)
    q_halves = jnp.transpose(queries, (0, 2, 3, 1, 4)).reshape(2, kv, group * half, hd)

    pref = page_table.shape[1]
    info = jnp.concatenate([page_table[0], cached_len, jnp.zeros((127 - pref,), jnp.int32)])
    info = jnp.broadcast_to(info[None], (8, 128))
    q_all, info_all = push([q_halves[0], info], "req", 1)
    keyval = jnp.dot(normed, w_keyval.reshape(width, kv * 2 * hd), preferred_element_type=f32)
    keyval = keyval.reshape(tok_rows, kv, 2 * hd)
    keys_new = jnp.transpose(rotate(keyval[..., :hd], angles).astype(bf16), (1, 0, 2))
    values_new = jnp.transpose(keyval[..., hd:].astype(bf16), (1, 0, 2))

    pages_dev, page = cache_pool.shape[0], cache_pool.shape[2]
    cap = (2 * pref + n_req - 1) // n_req
    table, lengths = info_all[:, 0, :pref], info_all[:, 0, pref]
    here = (table // pages_dev) == req_me
    entry = jnp.arange(pref, dtype=jnp.int32)
    earlier = (entry[None, :] < entry[:, None])[None]
    rank = jnp.sum((here[:, None, :] & earlier).astype(jnp.int32), axis=2)
    ranks = jnp.arange(cap, dtype=jnp.int32)[None, :, None]
    chosen = here[:, None, :] & (rank[:, None, :] == ranks)
    slots = jnp.sum(jnp.where(chosen, (table % pages_dev)[:, None, :], 0), axis=2)
    room = jnp.clip(lengths[:, None] - entry[None, :] * page, 0, page)
    valid = jnp.sum(jnp.where(chosen, room[:, None, :], 0), axis=2)
    shares, stats = owner_attend(slots, valid, q_all, cache_pool)
    shares, stats = push([shares, stats], "req", 2, scatter="lead")

    local_ok = (seg[:, None] == seg[None, :]) & (token[:, None] <= token[None, :])
    local_ok = local_ok.astype(f32)
    flags = jnp.tile(carried[:half].astype(f32), (group,))[None]
    ok = jnp.stack(
        [
            jnp.tile(local_ok[:, :half], (1, group)),
            jnp.tile(local_ok[:, half:], (1, group)),
            jnp.broadcast_to(flags, (tok_rows, group * half)),
        ]
    )
    context = merge(q_halves, keys_new, values_new, ok, shares, stats, group)
    (sums,) = push([jnp.dot(context, w_out, preferred_element_type=f32)], "tp", 3)
    resid = (hidden_in.astype(f32) + jnp.sum(sums, axis=0)).astype(bf16)
    moe_in = rms_scale(resid, moe_gain).astype(bf16)

    topk = expert_ids.shape[1]
    n_exp = n_req * w_gate_up.shape[0]
    cap_e = 4 * tok_rows * topk // (3 * n_exp)
    named = expert_ids[:, :, None] == jnp.arange(n_exp, dtype=jnp.int32)[None, None, :]
    member = jnp.any(named, axis=1)
    weight = jnp.sum(jnp.where(named, expert_weights[:, :, None], 0.0), axis=1)
    before = (token[None, :] < token[:, None]).astype(bf16)
    row = jnp.dot(before, member.astype(bf16), preferred_element_type=f32).astype(jnp.int32)
    at = jnp.where(member, row, -1)
    picks = at.T[:, None, :] == jnp.arange(cap_e, dtype=jnp.int32)[None, :, None]
    selector = picks.reshape(n_exp * cap_e, tok_rows).astype(bf16)
    share_in = lax.dynamic_slice_in_dim(moe_in, tp_me * part, part, axis=1)
    outgoing = jnp.dot(selector, share_in, preferred_element_type=f32).astype(bf16)
    (arrived,) = push([outgoing.reshape(n_exp, cap_e, part)], "req", 4, scatter="lead")
    (rows_all,) = push([arrived.reshape(n_exp * cap_e, part)], "tp", 5, place="cols")
    gate = jnp.dot(rows_all, w_gate_up[0, 0], preferred_element_type=f32)
    up = jnp.dot(rows_all, w_gate_up[0, 1], preferred_element_type=f32)
    act = (jax.nn.silu(gate) * up).astype(bf16)
    made = jnp.dot(act, w_down[0], preferred_element_type=f32).astype(bf16)
    (halves,) = push([made], "tp", 6, scatter="cols")
    summed = jnp.sum(halves.astype(f32), axis=0).astype(bf16).reshape(n_req, cap_e, part)
    (results,) = push([summed], "req", 7, scatter="lead")
    spread = jnp.where(picks, weight.T[:, None, :], 0.0).reshape(n_exp * cap_e, tok_rows)
    high = spread.astype(bf16)
    low = (spread - high.astype(f32)).astype(bf16)
    results = results.reshape(n_exp * cap_e, part)
    contract = (((0,), (0,)), ((), ()))
    moe_out = lax.dot_general(high, results, contract, preferred_element_type=f32)
    moe_out += lax.dot_general(low, results, contract, preferred_element_type=f32)
    resid_part = lax.dynamic_slice_in_dim(resid, tp_me * part, part, axis=1)
    final = (resid_part.astype(f32) + moe_out).astype(bf16)
    (layer_out,) = push([final], "tp", 8, place="cols")
    return layer_out


def solution(mesh):
    in_specs = (
        P("req", None),
        P(),
        P(None, "tp"),
        P(None, "tp", None),
        P("tp", None),
        P(),
        P("req", None, None, "tp"),
        P("req", "tp", None),
        P("req", None),
        P("req"),
        P("req", None),
        P("req", "tp", None, None),
        P("req", None),
        P("req", None),
    )
    out_specs = P("req", None)
    return jax.shard_map(shards, mesh=mesh, in_specs=in_specs, out_specs=out_specs, check_vma=False)
```

time: 567 us -> 497 us (0.88)
  Pallas kernels: 0 us -> 409 us
  waiting for transfers between devices: 309 us -> 0 us
  blocking collectives: 107 us -> 0 us
  local copies, waits for them, and re-layouts: 46.5 us -> 28.1 us
  starting transfers between devices: 14.3 us -> 0 us
  other arithmetic: 35.4 us -> 21.3 us
  between operations: 14.1 us -> 1.19 us
    pallas_call x0 -> x10, Pallas kernels: none -> 409 us  [the longest x8 393 us: push(): pl.pallas_call(functools.partial(push_kernel, axis, n, scatter, place, co...]
    all_to_all x2 -> x0, waiting for transfers between devices: 263 us -> none  [the longest x1 168 us: shards(): lax.all_to_all(served, 'req', split_axis=0, concat_axis=0, tiled=True)]
    all_to_all x2 -> x0, blocking collectives: 107 us -> none  [the longest x1 97.6 us: shards(): lax.all_to_all(outgoing, 'req', split_axis=0, concat_axis=0, tiled=True)]
    gather x3 -> x0, local copies, waits for them, and re-layouts: 23 us -> none  [the longest x1 9.82 us: shards(): results.reshape(-1, model_width)[assign_slot]]
    all_gather x1 -> x0, waiting for transfers between devices: 16.6 us -> none  [shards(): whole_rows = lax.all_gather(expert_share, 'tp', axis=0, tiled=True)]
    psum x1 -> x0, waiting for transfers between devices: 15.7 us -> none  [shards(): lax.psum(jnp.dot(context, w_out, preferred_element_type=jnp.float32), 'tp')]
    all_to_all x2 -> x0, starting transfers between devices: 14.1 us -> none  [the longest x1 7.61 us: shards(): lax.all_to_all(served, 'req', split_axis=0, concat_axis=0, tiled=True)]
    reduce_scatter x1 -> x0, waiting for transfers between devices: 13.8 us -> none  [shards(): lax.psum_scatter(jnp.dot(hidden_act, w_down[0], preferred_element_type=jn...]
  transfers between devices with their start and end apart: 5 -> 0, of which waited for: 5 -> 0; matrix products, arithmetic and copies ran while one was open for 4% -> 0% of each run, Pallas kernels for 0% -> 0%
where the time goes in v1:
time: 497 us; the launch traced here: 496 us
  Pallas kernels  409 us (82%)
  matrix products  36.5 us (7%)
  local copies, waits for them, and re-layouts  28.1 us (6%)
  other arithmetic  21.3 us (4%)
    pallas_call x8, Pallas kernels, push(): pl.pallas_call(functools.partial(push_kernel, axis, n, scatter, place, co...  393 us
    pallas_call x1, Pallas kernels, owner_attend(): pl.pallas_call(functools.partial(owner_kernel, cap, kv, 1.0 / math.sqrt(h...  15.1 us
    unnamed x47, local copies, waits for them, and re-layouts  12.8 us
    dot_general x1, matrix products, shards(): made = jnp.dot(act, w_down[0], preferred_element_type=f32).astype(bf16)  11.3 us

profile of v1, /device:TPU:15, one launch (start us, length us, event | category | flops | bytes accessed | tf_op | source)
XLA Modules:
  0.0 496.3 jit_solution(17770440257453634731)
XLA Ops:
  1.6 1.8 add_convert_fusion.2
  4.9 4.2 fusion.35
  10.9 1.8 maximum_bitcast_fusion
  14.5 56.7 %push_1.1 = (bf16[16,2,256,128]{3,2,1,0:T(8,128)(2,1)}, s32[16,8,128]{2,1,0:T(8,128)}) custom-call(bf16[2,256,128]{2,1,0:T(8,128)(2,1)} %bitcast.86, s32[8,128]{1,0:T(8,128)} %broadcast_in_dim.59.refs_1_), custom_call_target="tpu_custom_call" | custom-call | tf_op jit(solution)/shard_map/push_1/pallas_call | solution.py:83
  75.1 1.6 copy-done.2
  78.3 15.1 %owner_attend.1 = (bf16[16,2,128,256]{3,2,1,0:T(8,128)(2,1)S(1)}, f32[16,8,256]{2,1,0:T(8,128)S(1)}) custom-call(s32[16,4]{1,0:T(8,128)S(1)} %copy.49.slot_ref, s32[16,4]{1,0:T(8,128)S(1)} %copy.50.valid_ref, bf16[16,2,256,128]{3,2,1,0:T(8,128)(2,1)S(1)} %copy-done.4, bf16[16,2,128,256]{3,2,1,0:T(8,128)(2,1)S(1)} %copy-done.2), custom_call_target="tpu_custom_call" | custom-call | tf_op jit(solution)/shard_map/owner_attend/pallas_call | solution.py:133
  95.3 55.4 %push_2.1 = (bf16[16,2,128,256]{3,2,1,0:T(8,128)(2,1)}, f32[16,8,256]{2,1,0:T(8,128)}) custom-call(bf16[16,2,128,256]{3,2,1,0:T(8,128)(2,1)} %copy-done.5, f32[16,8,256]{2,1,0:T(8,128)} %copy-done.7), custom_call_target="tpu_custom_call" | custom-call | tf_op jit(solution)/shard_map/push_2/pallas_call | solution.py:83
  152.2 3.3 copy.53
  155.5 4.0 copy.43
  159.6 2.5 fusion.22
  171.7 3.9 fusion.49.refs_0_
  175.6 34.2 %push_3.1 = f32[2,128,2048]{2,1,0:T(8,128)} custom-call(f32[128,2048]{1,0:T(8,128)} %fusion.49.refs_0_), custom_call_target="tpu_custom_call" | custom-call | tf_op jit(solution)/shard_map/push_3/pallas_call | solution.py:83
  209.8 2.8 reduce_sum.89
  216.5 3.2 convolution_convert_fusion.1
  219.7 54.4 %push_4.1 = bf16[16,64,1024]{2,1,0:T(8,128)(2,1)} custom-call(bf16[16,64,1024]{2,1,0:T(8,128)(2,1)} %bitcast.80), custom_call_target="tpu_custom_call" | custom-call | tf_op jit(solution)/shard_map/push_4/pallas_call | solution.py:83
  274.1 65.5 %push_5.1 = bf16[1024,2048]{1,0:T(8,128)(2,1)} custom-call(bf16[1024,1024]{1,0:T(8,128)(2,1)} %bitcast.79), custom_call_target="tpu_custom_call" | custom-call | tf_op jit(solution)/shard_map/push_5/pallas_call | solution.py:83
  339.5 7.9 %fusion.1 = f32[1024,704]{0,1:T(8,128)} fusion(bf16[1024,2048]{1,0:T(8,128)(2,1)} %push_5.1, bf16[1,2,2048,704]{2,3,1,0:T(8,128)(2,1)} %param.20), kind=kOutput, calls=%fused_computation.2 | convolution fusion | flops 2952790016 | bytes 9961472 | tf_op jit(solution)/shard_map/dot_general | solution.py:311
  347.5 11.3 %convolution_convert_fusion.refs_0_ = bf16[1024,2048]{1,0:T(8,128)(2,1)} fusion(bf16[1,704,2048]{2,1,0:T(8,128)(2,1)S(1)} %copy-done, f32[1024,704]{0,1:T(8,128)} %fusion.1, bf16[1024,2048]{1,0:T(8,128)(2,1)} %push_5.1, bf16[1,2,2048,704]{2,3,1,0:T(8,128)(2,1)} %param.20), kind=kOutput, calls=%fused_computation | convolution fusion | flops 5912002560 | bytes 17039360 | tf_op jit(solution)/shard_map/dot_general | solution.py:313
  358.8 64.7 %push_6.1 = bf16[2,1024,1024]{2,1,0:T(8,128)(2,1)} custom-call(bf16[1024,2048]{1,0:T(8,128)(2,1)} %convolution_convert_fusion.refs_0_), custom_call_target="tpu_custom_call" | custom-call | tf_op jit(solution)/shard_map/push_6/pallas_call | solution.py:83
  423.5 5.2 %reduce_sum.92 = bf16[1024,1024]{1,0:T(8,128)(2,1)} reduce(bf16[2,1024,1024]{2,1,0:T(8,128)(2,1)} %push_6.1, bf16[]{:T(256)} %constant.67.clone.1), dimensions={0}, to_apply=%region_9.10 | reduce | flops 1048576 | bytes 6291458 | tf_op jit(solution)/shard_map/reduce_sum | solution.py:315
  428.6 51.8 %push_7.1 = bf16[16,64,1024]{2,1,0:T(8,128)(2,1)} custom-call(bf16[16,64,1024]{2,1,0:T(8,128)(2,1)} %bitcast.78), custom_call_target="tpu_custom_call" | custom-call | tf_op jit(solution)/shard_map/push_7/pallas_call | solution.py:83
  480.5 2.2 convolution_bitcast_fusion
  483.9 10.4 %push_8.1 = bf16[128,2048]{1,0:T(8,128)(2,1)} custom-call(bf16[128,1024]{1,0:T(8,128)(2,1)} %fusion.11.refs_0_), custom_call_target="tpu_custom_call" | custom-call | tf_op jit(solution)/shard_map/push_8/pallas_call | solution.py:83
  494.4 1.9 copy.60
  (94 shorter events, 29.2 us)
Async XLA Ops:
  0.0 347.5 %copy-start = (bf16[1,704,2048]{2,1,0:T(8,128)(2,1)S(1)}, bf16[1,704,2048]{2,1,0:T(8,128)(2,1)}, u32[]{:S(2)}) copy-start(bf16[1,704,2048]{2,1,0:T(8,128)(2,1)} %param.21) | copy-start | bytes 8650756
  9.1 4.7 copy-start.21
  12.7 62.2 %copy-start.11 = (bf16[2,2,4,64,128]{3,0,4,2,1:T(2,128)(2,1)}, bf16[2,2,4,64,128]{3,0,4,2,1:T(2,128)(2,1)S(1)}, u32[]{:S(2)}) copy-start(bf16[2,2,4,64,128]{3,0,4,2,1:T(2,128)(2,1)S(1)} %maximum_bitcast_fusion) | copy-start | bytes 786436
  75.1 1.6 copy-start.2
  76.7 1.6 copy-start.4
  93.4 1.3 copy-start.5
  94.7 0.6 copy-start.7
  155.5 4.0 copy-start.9
  155.5 4.0 copy-start.16
  159.5 2.5 copy-start.14
  159.5 2.5 copy-start.15
  159.5 5.4 %copy-start.18 = (s32[1,128]{1,0:T(1,128)S(1)}, s32[1,128]{1,0:T(1,128)}, u32[]{:S(2)}) copy-start(s32[1,128]{1,0:T(1,128)} %param.22) | copy-start | bytes 1540
  159.6 9.5 %copy-start.6 = (f32[16,8,256]{2,1,0:T(8,128)S(1)}, f32[16,8,256]{2,1,0:T(8,128)}, u32[]{:S(2)}) copy-start(f32[16,8,256]{2,1,0:T(8,128)} %get-tuple-element.16.stat_ref) | copy-start | bytes 393220
  169.0 1.6 copy-start.3
  175.6 37.1 %copy-start.10 = (bf16[128,2048]{1,0:T(8,128)(2,1)S(1)}, bf16[128,2048]{1,0:T(8,128)(2,1)}, u32[]{:S(2)}) copy-start(bf16[128,2048]{1,0:T(8,128)(2,1)} %param.14) | copy-start | bytes 1572868
  209.8 6.2 %copy-start.20 = (f32[2048]{0:T(1024)S(1)}, f32[2048]{0:T(1024)}, u32[]{:S(2)}) copy-start(f32[2048]{0:T(1024)} %param.19) | copy-start | bytes 24580
  209.8 6.2 %copy-start.17 = (s32[128,6]{0,1:T(8,128)S(1)}, s32[128,6]{0,1:T(8,128)}, u32[]{:S(2)}) copy-start(s32[128,6]{0,1:T(8,128)} %param.26) | copy-start | bytes 9220
  214.1 0.8 copy-start.12
  428.6 51.8 %copy-start.19 = (f32[128,6]{0,1:T(8,128)S(1)}, f32[128,6]{0,1:T(8,128)}, u32[]{:S(2)}) copy-start(f32[128,6]{0,1:T(8,128)} %param.27) | copy-start | bytes 9220
  428.6 54.1 %copy-start.13 = (bf16[128,2048]{1,0:T(8,128)(2,1)S(1)}, bf16[128,2048]{1,0:T(8,128)(2,1)}, u32[]{:S(2)}) copy-start(bf16[128,2048]{1,0:T(8,128)(2,1)} %copy-done.12) | copy-start | bytes 1572868
  480.5 2.3 copy-start.8
  480.5 15.8 %copy-start.1 = (bf16[1,704,2048]{2,1,0:T(8,128)(2,1)S(1)}, bf16[1,704,2048]{2,1,0:T(8,128)(2,1)}, u32[]{:S(2)}) copy-start(bf16[1,704,2048]{2,1,0:T(8,128)(2,1)} %param.21) | copy-start | bytes 8650756

commit v2 on v1

--- a/solution.py
+++ b/solution.py
@@ -83,14 +83,16 @@
     return pl.pallas_call(
         functools.partial(push_kernel, axis, n, scatter, place, count),
         out_shape=shapes,
-        in_specs=[pl.BlockSpec(memory_space=pl.ANY)] * count,
-        out_specs=[pl.BlockSpec(memory_space=pl.ANY)] * count,
+        in_specs=[pl.BlockSpec(memory_space=pltpu.VMEM)] * count,
+        out_specs=[pl.BlockSpec(memory_space=pltpu.VMEM)] * count,
         scratch_shapes=[
             pltpu.SemaphoreType.DMA((count, n)),
             pltpu.SemaphoreType.DMA((count, n)),
             pltpu.SemaphoreType.DMA((count,)),
         ],
-        compiler_params=pltpu.CompilerParams(collective_id=ident, has_side_effects=True),
+        compiler_params=pltpu.CompilerParams(
+            collective_id=ident, has_side_effects=True, vmem_limit_bytes=40 * 2**20
+        ),
         name="push_%d" % ident,
     )(*xs)
 

time: 497 us -> 329 us (0.66)
  Pallas kernels: 409 us -> 247 us
  matrix products: 36.5 us -> 28.7 us
    pallas_call x8, Pallas kernels: 393 us -> 231 us  [push(): pl.pallas_call(functools.partial(push_kernel, axis, n, scatter, place, co...]
    unnamed x47 -> x61, local copies, waits for them, and re-layouts: 12.8 us -> 19.9 us
where the time goes in v2:
time: 329 us; the launch traced here: 328 us
  Pallas kernels  247 us (75%)
  local copies, waits for them, and re-layouts  32.5 us (10%)
  matrix products  28.7 us (9%)
  other arithmetic  18.3 us (6%)
    pallas_call x8, Pallas kernels, push(): pl.pallas_call(functools.partial(push_kernel, axis, n, scatter, place, co...  231 us
    unnamed x61, local copies, waits for them, and re-layouts  19.9 us
    pallas_call x1, Pallas kernels, owner_attend(): pl.pallas_call(functools.partial(owner_kernel, cap, kv, 1.0 / math.sqrt(h...  15.1 us
    dot_general x1, matrix products, shards(): made = jnp.dot(act, w_down[0], preferred_element_type=f32).astype(bf16)  11.3 us

profile of v2, /device:TPU:15, one launch (start us, length us, event | category | flops | bytes accessed | tf_op | source)
XLA Modules:
  0.0 328.2 jit_solution(500267983345429686)
XLA Ops:
  1.6 1.8 add_convert_fusion.2
  5.0 4.2 %fusion.35 = f32[128,1024]{0,1:T(8,128)S(1)} fusion(bf16[2048,1024]{1,0:T(8,128)(2,1)} %param.16, bf16[128,2048]{1,0:T(8,128)(2,1)} %param.14, f32[2048]{0:T(1024)} %param.15, f32[128]{0:T(128)S(1)} %add_rsqrt_fusion.1), kind=kOutput, calls=%fused_computation.48 | convolution fusion | flops 537919488 | bytes 5251584 | tf_op jit(solution)/shard_map/reshape | solution.py:254
  9.6 1.6 maximum_bitcast_fusion
  12.5 56.2 %push_1.1 = (bf16[16,2,256,128]{3,2,1,0:T(8,128)(2,1)S(1)}, s32[16,8,128]{2,1,0:T(8,128)S(1)}) custom-call(bf16[2,256,128]{2,1,0:T(8,128)(2,1)S(1)} %bitcast.81, s32[8,128]{1,0:T(8,128)S(1)} %broadcast_in_dim.59.refs_1_), custom_call_target="tpu_custom_call" | custom-call | tf_op jit(solution)/shard_map/push_1/pallas_call | solution.py:83
  74.6 15.1 %owner_attend.1 = (bf16[16,2,128,256]{3,2,1,0:T(8,128)(2,1)S(1)}, f32[16,8,256]{2,1,0:T(8,128)S(1)}) custom-call(s32[16,4]{1,0:T(8,128)S(1)} %copy.49.slot_ref, s32[16,4]{1,0:T(8,128)S(1)} %copy.50.valid_ref, bf16[16,2,256,128]{3,2,1,0:T(8,128)(2,1)S(1)} %copy-done.10, bf16[16,2,128,256]{3,2,1,0:T(8,128)(2,1)S(1)} %copy-done.6), custom_call_target="tpu_custom_call" | custom-call | tf_op jit(solution)/shard_map/owner_attend/pallas_call | solution.py:135
  89.7 55.0 %push_2.1 = (bf16[16,2,128,256]{3,2,1,0:T(8,128)(2,1)S(1)}, f32[16,8,256]{2,1,0:T(8,128)S(1)}) custom-call(bf16[16,2,128,256]{3,2,1,0:T(8,128)(2,1)S(1)} %get-tuple-element.13.refs_0_, f32[16,8,256]{2,1,0:T(8,128)S(1)} %get-tuple-element.14.refs_1_), custom_call_target="tpu_custom_call" | custom-call | tf_op jit(solution)/shard_map/push_2/pallas_call | solution.py:83
  147.6 3.4 %copy.53 = bf16[256,8,2,256]{3,1,2,0:T(8,128)(2,1)} copy(bf16[256,8,2,256]{3,2,1,0:T(2,128)(2,1)} %bitcast.85) | data formatting | bytes 4194304
  150.9 4.0 %copy.43 = bf16[512,2048]{1,0:T(8,128)(2,1)} copy(bf16[512,2048]{0,1:T(8,128)(2,1)} %bitcast.83) | data formatting | bytes 4194304 | tf_op jit(solution)/shard_map/dot_general | solution.py:262
  155.0 2.5 fusion.22
  167.0 2.9 fusion.49.refs_0_
  170.0 3.7 %push_3.1 = f32[2,128,2048]{2,1,0:T(8,128)S(1)} custom-call(f32[128,2048]{1,0:T(8,128)S(1)} %fusion.49.refs_0_), custom_call_target="tpu_custom_call" | custom-call | tf_op jit(solution)/shard_map/push_3/pallas_call | solution.py:83
  175.0 2.8 reduce_sum.89
  181.7 2.0 convolution_convert_fusion.1
  183.7 52.0 %push_4.1 = bf16[16,64,1024]{2,1,0:T(8,128)(2,1)S(1)} custom-call(bf16[16,64,1024]{2,1,0:T(8,128)(2,1)S(1)} %bitcast.79), custom_call_target="tpu_custom_call" | custom-call | tf_op jit(solution)/shard_map/push_4/pallas_call | solution.py:83
  235.7 4.9 %push_5.1 = bf16[1024,2048]{1,0:T(8,128)(2,1)S(1)} custom-call(bf16[1024,1024]{1,0:T(8,128)(2,1)S(1)} %bitcast.78), custom_call_target="tpu_custom_call" | custom-call | tf_op jit(solution)/shard_map/push_5/pallas_call | solution.py:83
  240.6 1.9 copy-done.4
  242.6 4.8 %fusion.1 = f32[1024,704]{0,1:T(8,128)} fusion(bf16[1024,2048]{1,0:T(8,128)(2,1)S(1)} %push_5.1, bf16[1,2,2048,704]{2,3,1,0:T(8,128)(2,1)S(1)} %bitcast.99), kind=kOutput, calls=%fused_computation.2 | convolution fusion | flops 2952790016 | bytes 9961472 | tf_op jit(solution)/shard_map/dot_general | solution.py:313
  247.4 11.3 %convolution_convert_fusion.refs_0_ = bf16[1024,2048]{1,0:T(8,128)(2,1)} fusion(bf16[1,704,2048]{2,1,0:T(8,128)(2,1)S(1)} %copy-done, f32[1024,704]{0,1:T(8,128)} %fusion.1, bf16[1024,2048]{1,0:T(8,128)(2,1)} %copy-done.4, bf16[1,2,2048,704]{2,3,1,0:T(8,128)(2,1)} %param.20), kind=kOutput, calls=%fused_computation | convolution fusion | flops 5912002560 | bytes 17039360 | tf_op jit(solution)/shard_map/dot_general | solution.py:315
  258.7 2.2 copy-done.5
  260.9 4.2 %push_6.1 = bf16[2,1024,1024]{2,1,0:T(8,128)(2,1)S(1)} custom-call(bf16[1024,2048]{1,0:T(8,128)(2,1)S(1)} %copy-done.5), custom_call_target="tpu_custom_call" | custom-call | tf_op jit(solution)/shard_map/push_6/pallas_call | solution.py:83
  265.1 1.9 copy-done.2
  267.1 4.1 %reduce_sum.92 = bf16[1024,1024]{1,0:T(8,128)(2,1)S(1)} reduce(bf16[2,1024,1024]{2,1,0:T(8,128)(2,1)} %copy-done.2, bf16[]{:T(256)} %constant.67.clone.1), dimensions={0}, to_apply=%region_9.10 | reduce | flops 1048576 | bytes 6291458 | tf_op jit(solution)/shard_map/reduce_sum | solution.py:317
  271.2 53.3 %push_7.1 = bf16[16,64,1024]{2,1,0:T(8,128)(2,1)S(1)} custom-call(bf16[16,64,1024]{2,1,0:T(8,128)(2,1)S(1)} %bitcast.77), custom_call_target="tpu_custom_call" | custom-call | tf_op jit(solution)/shard_map/push_7/pallas_call | solution.py:83
  325.5 1.9 push_8.1
  (109 shorter events, 29.1 us)
Async XLA Ops:
  0.0 247.4 %copy-start = (bf16[1,704,2048]{2,1,0:T(8,128)(2,1)S(1)}, bf16[1,704,2048]{2,1,0:T(8,128)(2,1)}, u32[]{:S(2)}) copy-start(bf16[1,704,2048]{2,1,0:T(8,128)(2,1)} %param.21) | copy-start | bytes 8650756
  3.7 5.5 %copy-start.15 = (f32[128,64]{0,1:T(8,128)}, f32[128,64]{0,1:T(8,128)S(1)}, u32[]{:S(2)}) copy-start(f32[128,64]{0,1:T(8,128)S(1)} %get-tuple-element.32) | copy-start | bytes 98308
  3.7 5.5 %copy-start.17 = (f32[128,64]{0,1:T(8,128)}, f32[128,64]{0,1:T(8,128)S(1)}, u32[]{:S(2)}) copy-start(f32[128,64]{0,1:T(8,128)S(1)} %get-tuple-element.31) | copy-start | bytes 98308
  9.1 3.2 copy-start.26
  71.4 1.6 copy-start.6
  74.6 71.5 %copy-start.18 = (f32[128,64]{0,1:T(8,128)S(1)}, f32[128,64]{0,1:T(8,128)}, u32[]{:S(2)}) copy-start(f32[128,64]{0,1:T(8,128)} %copy-done.17) | copy-start | bytes 98308
  74.6 72.2 %copy-start.16 = (f32[128,64]{0,1:T(8,128)S(1)}, f32[128,64]{0,1:T(8,128)}, u32[]{:S(2)}) copy-start(f32[128,64]{0,1:T(8,128)} %copy-done.15) | copy-start | bytes 98308
  150.9 4.1 %copy-start.11 = (bf16[128,2048]{1,0:T(8,128)(2,1)S(1)}, bf16[128,2048]{1,0:T(8,128)(2,1)}, u32[]{:S(2)}) copy-start(bf16[128,2048]{1,0:T(8,128)(2,1)} %param.14) | copy-start | bytes 1572868
  150.9 4.1 %copy-start.21 = (f32[2048]{0:T(1024)S(1)}, f32[2048]{0:T(1024)}, u32[]{:S(2)}) copy-start(f32[2048]{0:T(1024)} %param.15) | copy-start | bytes 24580
  155.0 2.5 copy-start.19
  155.0 2.5 copy-start.20
  155.0 5.4 %copy-start.23 = (s32[1,128]{1,0:T(1,128)S(1)}, s32[1,128]{1,0:T(1,128)}, u32[]{:S(2)}) copy-start(s32[1,128]{1,0:T(1,128)} %param.22) | copy-start | bytes 1540
  164.4 1.6 copy-start.8
  169.9 7.9 %copy-start.12 = (bf16[128,2048]{1,0:T(8,128)(2,1)S(1)}, bf16[128,2048]{1,0:T(8,128)(2,1)}, u32[]{:S(2)}) copy-start(bf16[128,2048]{1,0:T(8,128)(2,1)} %param.14) | copy-start | bytes 1572868
  175.0 6.2 %copy-start.25 = (f32[2048]{0:T(1024)S(1)}, f32[2048]{0:T(1024)}, u32[]{:S(2)}) copy-start(f32[2048]{0:T(1024)} %param.19) | copy-start | bytes 24580
  175.0 6.2 %copy-start.22 = (s32[128,6]{0,1:T(8,128)S(1)}, s32[128,6]{0,1:T(8,128)}, u32[]{:S(2)}) copy-start(s32[128,6]{0,1:T(8,128)} %param.26) | copy-start | bytes 9220
  181.6 60.9 %slice-start = ((s8[5767168]{0:T(1024)(128)(4,1)}), s8[4194304]{0:T(1024)(128)(4,1)S(1)}, s32[]{:S(2)}) async-start(s8[5767168]{0:T(1024)(128)(4,1)} %bitcast.98), calls=%async_computation | async-start | bytes 8388608
  183.6 58.9 %slice-start.1 = ((s8[5767168]{0:T(1024)(128)(4,1)}), s8[1572864]{0:T(1024)(128)(4,1)S(1)}, s32[]{:S(2)}) async-start(s8[5767168]{0:T(1024)(128)(4,1)} %bitcast.98), calls=%async_computation.1 | async-start | bytes 3145728
  240.6 1.9 copy-start.4
  258.7 2.2 copy-start.5
  265.1 1.9 copy-start.2
  271.2 53.3 %copy-start.24 = (f32[128,6]{0,1:T(8,128)S(1)}, f32[128,6]{0,1:T(8,128)}, u32[]{:S(2)}) copy-start(f32[128,6]{0,1:T(8,128)} %param.27) | copy-start | bytes 9220
  271.2 53.8 %copy-start.14 = (bf16[128,2048]{1,0:T(8,128)(2,1)S(1)}, bf16[128,2048]{1,0:T(8,128)(2,1)}, u32[]{:S(2)}) copy-start(bf16[128,2048]{1,0:T(8,128)(2,1)} %copy-done.13) | copy-start | bytes 1572868
  324.5 3.7 %copy-start.1 = (bf16[1,704,2048]{2,1,0:T(8,128)(2,1)S(1)}, bf16[1,704,2048]{2,1,0:T(8,128)(2,1)}, u32[]{:S(2)}) copy-start(bf16[1,704,2048]{2,1,0:T(8,128)(2,1)} %param.21) | copy-start | bytes 8650756
  (5 other events, 6.4 us)
